TPU v7x, 32 devices: a whole 2x2x4 slice. The times are simulated.
32 devices in a mesh: brain: 2 (over x), slab: 16 (over z, y, core).
Axes of the slice: x: 2, y: 2, z: 4, core: 2. Of those that a mesh axis runs over, the one named last changes fastest.
Arguments:
- features: bfloat16 [32, 192, 16, 128], P(None, ('brain', 'slab')), parts along dimension 1, may hold values from -6 to 6
- conv_weight: bfloat16 [3, 128, 288], replicated, may hold values from -0.21875 to 0.21875
- norm_gain: float32 [4, 32], replicated, may hold values from 0.25 to 1.75
- norm_bias: float32 [4, 32], replicated, may hold values from -3 to 3
- head_weight: bfloat16 [4, 6, 32], replicated, may hold values from -2 to 2
- head_bias: float32 [4, 6], replicated, may hold values from -4 to 308
- patch_offsets: int32 [32, 2], P(('brain', 'slab')), parts along dimension 0, may hold values from -2 to 2
- fg_mask: int32 [32, 2], P(('brain', 'slab')), parts along dimension 0, may hold values 0 or 1
- acq_counts: int32 [32], P(('brain', 'slab')), parts along dimension 0, may hold values from 1 to 8, 64 in all
Outputs:
- resampled: float32 [6, 256, 16, 128], P(None, ('brain', 'slab')), parts along dimension 1
There are 2 independent parts, one for each index of `brain`. A program takes and returns all parts, laid end to end along the dimension named above; an argument that names none is the same for every part. Nothing has to cross between parts.
Inputs may be any that keep to these rules, and one draw needn't show every extreme that they name: `acq_counts`: within each brain volume separately, the 16 counts of that volume sum to 64 and some slab of that volume has exactly 8; the array of all volumes together sums to 64 once for every volume.
All inputs are finite; a program needn't handle non-finite values. No bound on the sum of `fg_mask` or of `acq_counts` on one device may be relied on, other than what follows from the above.
Results may differ from a plain program's by a relative error of at most 0.0003.
Values may be sent and summed in bfloat16 or wider, within the bound.
A program may use at most 64 MiB of HBM per device.

v0:
```python
import jax
import jax.numpy as jnp
from jax import lax
from jax.sharding import PartitionSpec as P

CLASSES = 6
MARGIN = 2
PATCHES = 2
PATCH_ROWS = 8
RIM = 4
PATCH_X = 10
MOST_ACQ = 8


prior_weight = 0.1


def with_halo(value, sides, width):
    for axis, dim in sides:
        size, length = (lax.axis_size(axis), value.shape[dim])
        up = [(i, (i + 1) % size) for i in range(size - 1)]
        down = [(j, i) for i, j in up]
        last = lax.slice_in_dim(value, length - width, length, axis=dim)
        leading = lax.slice_in_dim(value, 0, width, axis=dim)
        before = lax.ppermute(last, axis, up)
        after = lax.ppermute(leading, axis, down)
        value = jnp.concatenate([before, value, after], axis=dim)
    return value


def from_behind(value, axis, steps):
    count = lax.axis_size(axis)
    leading, last = (max(0, -steps), min(count, count - steps))
    return lax.ppermute(value, axis, [(source, source + steps) for source in range(leading, last)])


def gauss_line(length):
    positions = jnp.arange(length, dtype=jnp.float32)
    centre = (length - 1) / 2.0
    spread = length / 4.0
    scaled = (positions - centre) / spread
    return jnp.exp(-0.5 * scaled * scaled)


def patch_scores(patch, conv_weight, norm_gain, norm_bias, head_weight, head_bias):
    channels, length, row_span, column_count = patch.shape
    padded = jnp.pad(patch, ((0, 0), (1, 1), (1, 1), (0, 0)))
    zero_col = jnp.zeros(padded.shape[:-1] + (1,), padded.dtype)
    shifted = (
        jnp.concatenate([zero_col, padded[..., :-1]], -1),
        padded,
        jnp.concatenate([padded[..., 1:], zero_col], -1),
    )
    tap_list = [
        source[:, :, row_shift : row_shift + row_span]
        for row_shift in range(3)
        for source in shifted
    ]
    stacked = jnp.concatenate(tap_list, 0)
    conv_out = jnp.zeros((conv_weight.shape[1], length * row_span * column_count), jnp.float32)
    for depth_tap in range(3):
        sliced = stacked[:, depth_tap : depth_tap + length].reshape(9 * channels, -1)
        conv_out = conv_out + jnp.dot(
            conv_weight[depth_tap], sliced, preferred_element_type=jnp.float32
        )
    centre_mean = jnp.mean(conv_out, axis=1, keepdims=True)
    centred = conv_out - centre_mean
    variance = jnp.mean(centred * centred, axis=1, keepdims=True)
    normed = (
        centred * lax.rsqrt(variance + 1e-05) * norm_gain.reshape(-1)[:, None]
        + norm_bias.reshape(-1)[:, None]
    )
    activated = jnp.where(normed > 0, normed, 0.01 * normed)
    fold_count = head_weight.shape[0]
    logits = (
        jnp.einsum(
            "fkc,fcv->fkv",
            head_weight.astype(jnp.float32),
            activated.reshape(fold_count, channels, -1),
            precision=lax.Precision.HIGHEST,
        )
        + head_bias[:, :, None]
    )
    class_probs = jnp.sum(jax.nn.softmax(logits, axis=1), axis=0) / fold_count
    window = (
        gauss_line(length)[:, None, None]
        * gauss_line(row_span)[None, :, None]
        * gauss_line(column_count)[None, None, :]
    ).reshape(-1)
    weighted = (class_probs * window[None, :]).reshape(-1, length, row_span, column_count)
    return (weighted, window.reshape(length, row_span, column_count))


def local(
    features,
    conv_weight,
    norm_gain,
    norm_bias,
    head_weight,
    head_bias,
    patch_offsets,
    fg_mask,
    acq_counts,
):
    channels, planes, row_total, column_count = features.shape
    slab_count = lax.axis_size("slab")
    slab_index = lax.axis_index("slab")
    extended = with_halo(features, (("slab", 1),), RIM)
    span_planes = planes + 2 * RIM
    prob_parts = []
    weight_parts = []
    for patch_index in range(PATCHES):
        row_first = patch_index * PATCH_ROWS
        patch_start = RIM - MARGIN + patch_offsets[0, patch_index]
        patch = lax.dynamic_slice_in_dim(
            extended[:, :, row_first : row_first + PATCH_ROWS], patch_start, PATCH_X, 1
        )
        keep_mask = fg_mask[0, patch_index]

        def scored(patch=patch):
            return patch_scores(patch, conv_weight, norm_gain, norm_bias, head_weight, head_bias)

        class_probs, window = scored()
        keep_value = keep_mask.astype(jnp.float32)
        class_probs = class_probs * keep_value
        window = window * keep_value
        placed_probs = jnp.zeros((CLASSES, span_planes, PATCH_ROWS, column_count), jnp.float32)
        placed_weights = jnp.zeros((span_planes, PATCH_ROWS, column_count), jnp.float32)
        prob_parts.append(
            lax.dynamic_update_slice_in_dim(placed_probs, class_probs, patch_start, 1)
        )
        weight_parts.append(lax.dynamic_update_slice_in_dim(placed_weights, window, patch_start, 0))
    prob_sums = jnp.concatenate(prob_parts, 2)
    weight_sums = jnp.concatenate(weight_parts, 1)
    extra_plane = 1
    from_above = from_behind(
        (prob_sums[:, : RIM + extra_plane], weight_sums[: RIM + extra_plane]), "slab", -1
    )
    from_below = from_behind(
        (prob_sums[:, RIM + planes - extra_plane :], weight_sums[RIM + planes - extra_plane :]),
        "slab",
        1,
    )
    pad_low = ((0, 0), (0, planes - RIM), (0, 0), (0, 0))
    pad_high = ((0, 0), (planes - RIM, 0), (0, 0), (0, 0))
    total_probs = (
        prob_sums[:, RIM : RIM + planes]
        + jnp.pad(from_below[0][:, extra_plane:], pad_low)
        + jnp.pad(from_above[0][:, :RIM], pad_high)
    )
    total_weights = (
        weight_sums[RIM : RIM + planes]
        + jnp.pad(from_below[1][extra_plane:], pad_low[1:])
        + jnp.pad(from_above[1][:RIM], pad_high[1:])
    )
    background = (jnp.arange(CLASSES) == 0).astype(jnp.float32)[:, None, None, None] * prior_weight
    merged = (total_probs + background) / (total_weights + prior_weight)
    below_plane = (from_below[0][:, 0] + prob_sums[:, RIM - 1] + background[:, 0]) / (
        from_below[1][0] + weight_sums[RIM - 1] + prior_weight
    )
    above_plane = (from_above[0][:, RIM] + prob_sums[:, RIM + planes] + background[:, 0]) / (
        from_above[1][RIM] + weight_sums[RIM + planes] + prior_weight
    )
    edged = jnp.concatenate([below_plane[:, None], merged, above_plane[:, None]], 1)
    acq_count = acq_counts[0].astype(jnp.float32)
    slot_ids = jnp.arange(MOST_ACQ, dtype=jnp.float32)
    step_size = planes / jnp.maximum(acq_count - 1.0, 1.0)
    local_pos = slot_ids * step_size - 0.5
    slab_anchor = (slab_index * planes).astype(jnp.float32)
    global_pos = jnp.clip(slab_anchor + local_pos, 0.0, float(slab_count * planes - 1))
    local_pos = global_pos - slab_anchor
    plane_pos = jnp.arange(planes + 2, dtype=jnp.float32) - 1.0
    used = (slot_ids < acq_count).astype(jnp.float32)
    resample_matrix = (
        jnp.maximum(0.0, 1.0 - jnp.abs(local_pos[:, None] - plane_pos[None, :])) * used[:, None]
    )
    return jnp.einsum("kj,cjhw->ckhw", resample_matrix, edged, precision=lax.Precision.HIGHEST)


def solution(mesh):
    in_specs = (
        P(None, ("brain", "slab"), None, None),
        P(),
        P(),
        P(),
        P(),
        P(),
        P(("brain", "slab"), None),
        P(("brain", "slab"), None),
        P(("brain", "slab")),
    )
    out_specs = P(None, ("brain", "slab"), None, None)
    return jax.shard_map(local, mesh=mesh, in_specs=in_specs, out_specs=out_specs, check_vma=False)
```

profile of v0, /device:TPU:11, one launch (start us, length us, event | category | flops | bytes accessed | tf_op | source)
XLA Modules:
  0.0 93.2 jit_solution(6910389079511696735)
XLA Ops:
  0.0 1.4 %fusion.107 = (bf16[32,4,16,128]{3,2,1,0:T(8,128)(2,1)S(1)}, bf16[32,4,16,128]{3,2,1,0:T(8,128)(2,1)S(1)}) fusion(bf16[32,6,16,128]{3,2,1,0:T(8,128)(2,1)} %param.9), kind=kLoop, calls=%fused_computation.184 | loop fusion | bytes 2097152 | tf_op jit(solution)/shard_map/slice | solution.py:24
  1.4 3.7 %collective-permute-start = (bf16[32,4,16,128]{3,2,1,0:T(8,128)(2,1)S(1)}, bf16[32,4,16,128]{3,2,1,0:T(8,128)(2,1)S(1)}, u32[]{:S(2)}, u32[]{:S(2)}) collective-permute-start(bf16[32,4,16,128]{3,2,1,0:T(8,128)(2,1)S(1)} %get-tuple-element.18), channel_id=1, source_target_pairs={{0,1},{1,2},{2,3},{3,4},{4,5},{5,6},{6,7},{7,8},{8,9},{9,10},{10,1... | collective-permute-start | bytes 1572872 | tf_op jit(solution)/shard_map/ppermute | solution.py:25
  5.1 1.9 %collective-permute-start.1 = (bf16[32,4,16,128]{3,2,1,0:T(8,128)(2,1)S(1)}, bf16[32,4,16,128]{3,2,1,0:T(8,128)(2,1)S(1)}, u32[]{:S(2)}, u32[]{:S(2)}) collective-permute-start(bf16[32,4,16,128]{3,2,1,0:T(8,128)(2,1)S(1)} %get-tuple-element.17), channel_id=1, source_target_pairs={{1,0},{2,1},{3,2},{4,3},{5,4},{6,5},{7,6},{8,7},{9,8},{10,9},{11,1... | collective-permute-start | bytes 1572872 | tf_op jit(solution)/shard_map/ppermute | solution.py:26
  7.1 1.4 %fusion.109 = (s32[1,1]{1,0:T(1,128)}, s32[1,1]{1,0:T(1,128)}) fusion(s32[1,2]{1,0:T(1,128)} %param.15), kind=kLoop, calls=%fused_computation.186 | loop fusion | bytes 16 | tf_op jit(solution)/shard_map/slice | solution.py:114
  11.0 1.4 %fusion.108 = (s32[1,1]{1,0:T(1,128)}, s32[1,1]{1,0:T(1,128)}) fusion(s32[1,2]{1,0:T(1,128)} %param.16), kind=kLoop, calls=%fused_computation.185 | loop fusion | bytes 16 | tf_op jit(solution)/shard_map/slice | solution.py:118
  13.7 0.1 broadcast_multiply_fusion
  13.7 0.1 fusion.77
  13.8 0.1 fusion.78
  13.9 3.6 %collective-permute-start.3 = (f32[5,16,128]{2,1,0:T(8,128)S(1)}, f32[5,16,128]{2,1,0:T(8,128)S(1)}, u32[]{:S(2)}, u32[]{:S(2)}) collective-permute-start(f32[5,16,128]{2,1,0:T(8,128)S(1)} %get-tuple-element.25), channel_id=1, source_target_pairs={{0,1},{1,2},{2,3},{3,4},{4,5},{5,6},{6,7},{7,8},{8,9},{9,10},{10,1... | collective-permute-start | bytes 122888 | tf_op jit(solution)/shard_map/ppermute | solution.py:34
  17.6 1.9 %collective-permute-start.5 = (f32[5,16,128]{2,1,0:T(8,128)S(1)}, f32[5,16,128]{2,1,0:T(8,128)S(1)}, u32[]{:S(2)}, u32[]{:S(2)}) collective-permute-start(f32[5,16,128]{2,1,0:T(8,128)S(1)} %get-tuple-element.26), channel_id=1, source_target_pairs={{1,0},{2,1},{3,2},{4,3},{5,4},{6,5},{7,6},{8,7},{9,8},{10,9},{11,1... | collective-permute-start | bytes 122888 | tf_op jit(solution)/shard_map/ppermute | solution.py:34
  20.3 0.8 add.231
  21.0 0.8 mul.311
  21.8 1.1 %collective-permute-done.5 = f32[5,16,128]{2,1,0:T(8,128)S(1)} collective-permute-done((f32[5,16,128]{2,1,0:T(8,128)S(1)}, f32[5,16,128]{2,1,0:T(8,128)S(1)}, u32[]{:S(2)}, u32[]{:S(2)}) %collective-permute-start.5) | collective-permute-done | bytes 40992 | tf_op jit(solution)/shard_map/ppermute | solution.py:34
  23.0 1.3 %constant_dynamic-update-slice_fusion.1 = bf16[32,14,16,128]{3,2,1,0:T(8,128)(2,1)S(1)} fusion(bf16[32,14,16,128]{3,2,1,0:T(8,128)(2,1)S(1)} %constant_dynamic-update-slice_fusion.2, bf16[32,6,16,128]{3,2,1,0:T(8,128)(2,1)} %param.9), kind=kLoop, calls=%fused_computation.137 | loop fusion | bytes 1572864
  24.3 0.1 constant_dynamic-update-slice_fusion
  24.4 0.3 fusion.106
  24.7 0.1 constant_dynamic-slice_fusion
  24.8 1.1 %pad_slice_fusion.2 = (bf16[32,12,10,127]{3,2,1,0:T(8,128)(2,1)S(1)}, bf16[32,12,10,127]{3,2,1,0:T(8,128)(2,1)S(1)}) fusion(bf16[32,10,8,128]{3,2,1,0:T(8,128)(2,1)S(1)} %get-tuple-element.41), kind=kLoop, calls=%fused_computation.38 | loop fusion | bytes 2606080 | tf_op jit(solution)/shard_map/slice | solution.py:52
  26.0 0.3 fusion.32
  26.3 0.2 fusion.41
  26.5 0.2 fusion.35
  26.7 0.7 fusion.33
  27.4 0.1 fusion.42
  27.5 0.4 fusion.36
  27.9 0.7 fusion.34
  28.6 0.2 fusion.43
  28.8 0.4 fusion.37
  29.3 3.3 %fusion.105 = (bf16[288,10,8,128]{3,2,1,0:T(8,128)(2,1)S(1)}, bf16[288,10,8,128]{3,2,1,0:T(8,128)(2,1)S(1)}, bf16[288,10,8,128]{3,2,1,0:T(8,128)(2,1)S(1)}) fusion(bf16[288,12,8,128]{3,2,1,0:T(8,128)(2,1)S(1)} %fusion.37), kind=kLoop, calls=%fused_computation.182 | loop fusion | bytes 35389440 | tf_op jit(solution)/shard_map/slice | solution.py:62
  32.6 1.7 %fusion.16 = f32[10240,128]{0,1:T(8,128)S(1)} fusion(bf16[36,8,80,128]{3,2,1,0:T(8,128)(2,1)S(1)} %bitcast.99, bf16[3,128,288]{1,2,0:T(8,128)(2,1)S(1)} %copy-done.1), kind=kOutput, calls=%fused_computation.24 | convolution fusion | flops 754974720 | bytes 11214848 | tf_op jit(solution)/shard_map/dot_general | solution.py:63
  34.3 2.0 %convolution_add_fusion.1 = f32[10240,128]{0,1:T(8,128)S(1)} fusion(f32[10240,128]{0,1:T(8,128)S(1)} %fusion.16, bf16[36,8,80,128]{3,2,1,0:T(8,128)(2,1)S(1)} %bitcast.97, bf16[3,128,288]{1,2,0:T(8,128)(2,1)S(1)} %copy-done.1), kind=kOutput, calls=%fused_computation.7 | convolution fusion | flops 756285440 | bytes 16457728 | tf_op jit(solution)/shard_map/dot_general | solution.py:63
  36.3 1.8 %fusion.111 = (f32[128]{0:T(128)S(1)}, f32[10240,128]{0,1:T(8,128)S(1)}) fusion(f32[10240,128]{0,1:T(8,128)S(1)} %convolution_add_fusion.1, bf16[3,128,288]{1,2,0:T(8,128)(2,1)S(1)} %copy-done.1, bf16[36,8,80,128]{3,2,1,0:T(8,128)(2,1)S(1)} %bitcast.95), kind=kOutput, calls=%fused_computation.188 | convolution fusion | flops 757596032 | bytes 16458240 | tf_op jit(solution)/shard_map/dot_general | solution.py:63
  38.1 0.7 multiply_reduce_fusion
  38.8 1.1 %pad_slice_fusion.7 = (bf16[32,12,10,127]{3,2,1,0:T(8,128)(2,1)S(1)}, bf16[32,12,10,127]{3,2,1,0:T(8,128)(2,1)S(1)}) fusion(bf16[32,10,8,128]{3,2,1,0:T(8,128)(2,1)S(1)} %get-tuple-element.42), kind=kLoop, calls=%fused_computation.43 | loop fusion | bytes 2606080 | tf_op jit(solution)/shard_map/slice | solution.py:52
  40.0 0.3 fusion.26
  40.3 0.2 fusion.38
  40.5 0.2 fusion.29
  40.7 0.7 fusion.27
  41.4 0.1 fusion.39
  41.5 0.4 fusion.30
  41.9 0.7 fusion.28
  42.6 0.2 fusion.40
  42.8 0.4 fusion.31
  43.3 4.9 %fusion.104 = (bf16[288,10,8,128]{3,2,1,0:T(8,128)(2,1)S(1)}, bf16[288,10,8,128]{3,2,1,0:T(8,128)(2,1)}, bf16[288,10,8,128]{3,2,1,0:T(8,128)(2,1)S(1)}) fusion(bf16[288,12,8,128]{3,2,1,0:T(8,128)(2,1)S(1)} %fusion.31), kind=kLoop, calls=%fused_computation.181 | loop fusion | bytes 35389440 | tf_op jit(solution)/shard_map/slice | solution.py:62
  48.2 1.7 %fusion.23 = f32[10240,128]{0,1:T(8,128)S(1)} fusion(bf16[36,8,80,128]{3,2,1,0:T(8,128)(2,1)S(1)} %bitcast.100, bf16[3,128,288]{1,2,0:T(8,128)(2,1)S(1)} %copy-done.1), kind=kOutput, calls=%fused_computation.31 | convolution fusion | flops 754974720 | bytes 11214848 | tf_op jit(solution)/shard_map/dot_general | solution.py:63
  49.9 4.4 %convolution_add_fusion.3 = f32[10240,128]{0,1:T(8,128)S(1)} fusion(f32[10240,128]{0,1:T(8,128)S(1)} %fusion.23, bf16[36,8,80,128]{3,2,1,0:T(8,128)(2,1)} %bitcast.98, bf16[3,128,288]{1,2,0:T(8,128)(2,1)S(1)} %copy-done.1), kind=kOutput, calls=%fused_computation.9 | convolution fusion | flops 756285440 | bytes 16457728 | tf_op jit(solution)/shard_map/dot_general | solution.py:63
  54.3 1.8 %fusion.110 = (f32[128]{0:T(128)S(1)}, f32[10240,128]{0,1:T(8,128)S(1)}) fusion(f32[10240,128]{0,1:T(8,128)S(1)} %convolution_add_fusion.3, bf16[3,128,288]{1,2,0:T(8,128)(2,1)S(1)} %copy-done.1, bf16[36,8,80,128]{3,2,1,0:T(8,128)(2,1)S(1)} %bitcast.96), kind=kOutput, calls=%fused_computation.187 | convolution fusion | flops 757596032 | bytes 16458240 | tf_op jit(solution)/shard_map/dot_general | solution.py:63
  56.1 0.7 multiply_reduce_fusion.1
  56.8 4.1 %compare_select_fusion.1 = (f32[128,10240]{1,0:T(8,128)}, f32[128,10240]{1,0:T(8,128)S(1)}) fusion(f32[10240,128]{0,1:T(8,128)S(1)} %get-tuple-element.38, f32[128]{0:T(128)S(1)} %add.231, f32[128]{0:T(128)S(1)} %mul.311, f32[128]{0:T(128)S(1)} %add_rsqrt_fusion.1, f32[128]{0:T(128)S(1)} %broadcast_multiply_fusion.2, f32[128]{0:T(128)S(1)} %add_rsqrt_fusion, ...), kind=kLoop, calls=%fused_computation.5 | loop fusion | flops 18350080 | bytes 20974592 | tf_op jit(solution)/shard_map/jit(_where)/select_n | solution.py:73
  61.0 1.9 %fusion.10 = f32[4,6,10240]{2,1,0:T(8,128)S(1)} fusion(f32[4,32,10240]{2,1,0:T(8,128)S(1)} %bitcast.102, f32[4,6]{1,0:T(4,128)S(1)} %copy-done.6, bf16[4,6,32]{2,0,1:T(4,128)(2,1)S(1)} %copy-done), kind=kOutput, calls=%fused_computation.17 | convolution fusion | flops 94617600 | bytes 6227552 | tf_op jit(solution)/shard_map/fkc,fcv->fkv/dot_general | solution.py:76
  62.9 0.9 fusion.113
  63.9 4.4 %fusion.11 = f32[4,6,10240]{2,1,0:T(8,128)S(1)} fusion(f32[4,32,10240]{2,1,0:T(8,128)} %bitcast.101, f32[4,6]{1,0:T(4,128)S(1)} %copy-done.6, bf16[4,6,32]{2,0,1:T(4,128)(2,1)S(1)} %copy-done), kind=kOutput, calls=%fused_computation.19 | convolution fusion | flops 94617600 | bytes 6227552 | tf_op jit(solution)/shard_map/fkc,fcv->fkv/dot_general | solution.py:76
  68.3 0.9 fusion.112
  69.3 0.1 fusion.57
  69.4 3.5 %dynamic_update_slice.12 = f32[6,14,8,128]{3,1,2,0:T(8,128)S(1)} dynamic-update-slice(f32[6,14,8,128]{3,1,2,0:T(8,128)S(1)} %broadcast.272.clone.1, f32[6,10,8,128]{3,1,2,0:T(8,128)S(1)} %get-tuple-element.27, s32[]{:T(128)} %constant.30.clone.1, s32[]{:T(128)S(6)} %select_n.17, s32[]{:T(128)} %constant.30.clone.1, s32[]{:T(128)} %constant.30.clone.1) | dynamic-update-slice | bytes 491524 | tf_op jit(solution)/shard_map/dynamic_update_slice | solution.py:130
  72.9 3.5 %dynamic_update_slice.13 = f32[6,14,8,128]{3,1,2,0:T(8,128)S(1)} dynamic-update-slice(f32[6,14,8,128]{3,1,2,0:T(8,128)S(1)} %broadcast.272.clone, f32[6,10,8,128]{3,1,2,0:T(8,128)S(1)} %get-tuple-element.28, s32[]{:T(128)} %constant.30.clone.1, s32[]{:T(128)S(6)} %select_n.19, s32[]{:T(128)} %constant.30.clone.1, s32[]{:T(128)} %constant.30.clone.1) | dynamic-update-slice | bytes 491524 | tf_op jit(solution)/shard_map/dynamic_update_slice | solution.py:130
  76.4 0.1 fusion.45
  76.5 2.6 %collective-permute-start.2 = (f32[6,5,16,128]{3,1,2,0:T(8,128)S(1)}, f32[6,5,16,128]{3,1,2,0:T(8,128)S(1)}, u32[]{:S(2)}, u32[]{:S(2)}) collective-permute-start(f32[6,5,16,128]{3,1,2,0:T(8,128)S(1)} %get-tuple-element.15), channel_id=1, source_target_pairs={{0,1},{1,2},{2,3},{3,4},{4,5},{5,6},{6,7},{7,8},{8,9},{9,10},{10,1... | collective-permute-start | bytes 737288 | tf_op jit(solution)/shard_map/ppermute | solution.py:34
  79.1 2.7 %collective-permute-start.4 = (f32[6,5,16,128]{3,1,2,0:T(8,128)S(1)}, f32[6,5,16,128]{3,1,2,0:T(8,128)S(1)}, u32[]{:S(2)}, u32[]{:S(2)}) collective-permute-start(f32[6,5,16,128]{3,1,2,0:T(8,128)S(1)} %get-tuple-element.16), channel_id=1, source_target_pairs={{1,0},{2,1},{3,2},{4,3},{5,4},{6,5},{7,6},{8,7},{9,8},{10,9},{11,1... | collective-permute-start | bytes 737288 | tf_op jit(solution)/shard_map/ppermute | solution.py:34
  81.8 1.9 %collective-permute-done.2 = f32[6,5,16,128]{3,1,2,0:T(8,128)S(1)} collective-permute-done((f32[6,5,16,128]{3,1,2,0:T(8,128)S(1)}, f32[6,5,16,128]{3,1,2,0:T(8,128)S(1)}, u32[]{:S(2)}, u32[]{:S(2)}) %collective-permute-start.2) | collective-permute-done | bytes 245792 | tf_op jit(solution)/shard_map/ppermute | solution.py:34
  83.8 7.6 %collective-permute-done.4 = f32[6,5,16,128]{3,1,2,0:T(8,128)S(1)} collective-permute-done((f32[6,5,16,128]{3,1,2,0:T(8,128)S(1)}, f32[6,5,16,128]{3,1,2,0:T(8,128)S(1)}, u32[]{:S(2)}, u32[]{:S(2)}) %collective-permute-start.4) | collective-permute-done | bytes 245792 | tf_op jit(solution)/shard_map/ppermute | solution.py:34
  91.5 0.1 fusion.50
  91.6 0.2 add_divide_fusion.1
  91.8 0.6 convolution_bitcast_fusion
  92.4 0.8 copy.21
  (45 shorter events, 0.5 us)
Async XLA Ops:
  0.0 61.0 %copy-start = (bf16[4,6,32]{2,0,1:T(4,128)(2,1)S(1)}, bf16[4,6,32]{2,0,1:T(4,128)(2,1)}, u32[]{:S(2)}) copy-start(bf16[4,6,32]{2,0,1:T(4,128)(2,1)} %param.13) | copy-start | bytes 4612
  1.4 21.5 %collective-permute-start = (bf16[32,4,16,128]{3,2,1,0:T(8,128)(2,1)S(1)}, bf16[32,4,16,128]{3,2,1,0:T(8,128)(2,1)S(1)}, u32[]{:S(2)}, u32[]{:S(2)}) collective-permute-start(bf16[32,4,16,128]{3,2,1,0:T(8,128)(2,1)S(1)} %get-tuple-element.18), channel_id=1, source_target_pairs={{0,1},{1,2},{2,3},{3,4},{4,5},{5,6},{6,7},{7,8},{8,9},{9,10},{10,1... | collective-permute-start | bytes 1572872 | tf_op jit(solution)/shard_map/ppermute | solution.py:25
  5.1 19.2 %collective-permute-start.1 = (bf16[32,4,16,128]{3,2,1,0:T(8,128)(2,1)S(1)}, bf16[32,4,16,128]{3,2,1,0:T(8,128)(2,1)S(1)}, u32[]{:S(2)}, u32[]{:S(2)}) collective-permute-start(bf16[32,4,16,128]{3,2,1,0:T(8,128)(2,1)S(1)} %get-tuple-element.17), channel_id=1, source_target_pairs={{1,0},{2,1},{3,2},{4,3},{5,4},{6,5},{7,6},{8,7},{9,8},{10,9},{11,1... | collective-permute-start | bytes 1572872 | tf_op jit(solution)/shard_map/ppermute | solution.py:26
  13.9 7.9 %collective-permute-start.3 = (f32[5,16,128]{2,1,0:T(8,128)S(1)}, f32[5,16,128]{2,1,0:T(8,128)S(1)}, u32[]{:S(2)}, u32[]{:S(2)}) collective-permute-start(f32[5,16,128]{2,1,0:T(8,128)S(1)} %get-tuple-element.25), channel_id=1, source_target_pairs={{0,1},{1,2},{2,3},{3,4},{4,5},{5,6},{6,7},{7,8},{8,9},{9,10},{10,1... | collective-permute-start | bytes 122888 | tf_op jit(solution)/shard_map/ppermute | solution.py:34
  17.6 5.3 %collective-permute-start.5 = (f32[5,16,128]{2,1,0:T(8,128)S(1)}, f32[5,16,128]{2,1,0:T(8,128)S(1)}, u32[]{:S(2)}, u32[]{:S(2)}) collective-permute-start(f32[5,16,128]{2,1,0:T(8,128)S(1)} %get-tuple-element.26), channel_id=1, source_target_pairs={{1,0},{2,1},{3,2},{4,3},{5,4},{6,5},{7,6},{8,7},{9,8},{10,9},{11,1... | collective-permute-start | bytes 122888 | tf_op jit(solution)/shard_map/ppermute | solution.py:34
  21.8 4.1 %copy-start.2 = (f32[5,16,128]{2,1,0:T(8,128)}, f32[5,16,128]{2,1,0:T(8,128)S(1)}, u32[]{:S(2)}) copy-start(f32[5,16,128]{2,1,0:T(8,128)S(1)} %collective-permute-done.3) | copy-start | bytes 122884
  22.9 3.0 %copy-start.4 = (f32[5,16,128]{2,1,0:T(8,128)}, f32[5,16,128]{2,1,0:T(8,128)S(1)}, u32[]{:S(2)}) copy-start(f32[5,16,128]{2,1,0:T(8,128)S(1)} %collective-permute-done.5) | copy-start | bytes 122884
  29.3 3.3 %copy-start.1 = (bf16[3,128,288]{1,2,0:T(8,128)(2,1)S(1)}, bf16[3,128,288]{1,2,0:T(8,128)(2,1)}, u32[]{:S(2)}) copy-start(bf16[3,128,288]{1,2,0:T(8,128)(2,1)} %param.10) | copy-start | bytes 663556
  56.8 4.2 %copy-start.6 = (f32[4,6]{1,0:T(4,128)S(1)}, f32[4,6]{1,0:T(4,128)}, u32[]{:S(2)}) copy-start(f32[4,6]{1,0:T(4,128)} %param.14) | copy-start | bytes 292
  68.3 13.5 %slice-start = ((f32[5,16,128]{2,1,0:T(8,128)}), f32[4,16,128]{2,1,0:T(8,128)S(1)}, s32[]{:S(2)}) async-start(f32[5,16,128]{2,1,0:T(8,128)} %copy-done.2), calls=%async_computation | async-start | bytes 65536 | tf_op jit(solution)/shard_map/slice | solution.py:153
  68.3 13.5 %slice-start.1 = ((f32[5,16,128]{2,1,0:T(8,128)}), f32[4,16,128]{2,1,0:T(8,128)S(1)}, s32[]{:S(2)}) async-start(f32[5,16,128]{2,1,0:T(8,128)} %copy-done.4), calls=%async_computation.1 | async-start | bytes 65536 | tf_op jit(solution)/shard_map/slice | solution.py:154
  68.3 13.5 %copy-start.3 = (f32[5,16,128]{2,1,0:T(8,128)S(1)}, f32[5,16,128]{2,1,0:T(8,128)}, u32[]{:S(2)}) copy-start(f32[5,16,128]{2,1,0:T(8,128)} %copy-done.2) | copy-start | bytes 122884
  68.3 13.5 %copy-start.5 = (f32[5,16,128]{2,1,0:T(8,128)S(1)}, f32[5,16,128]{2,1,0:T(8,128)}, u32[]{:S(2)}) copy-start(f32[5,16,128]{2,1,0:T(8,128)} %copy-done.4) | copy-start | bytes 122884
  76.5 7.3 %collective-permute-start.2 = (f32[6,5,16,128]{3,1,2,0:T(8,128)S(1)}, f32[6,5,16,128]{3,1,2,0:T(8,128)S(1)}, u32[]{:S(2)}, u32[]{:S(2)}) collective-permute-start(f32[6,5,16,128]{3,1,2,0:T(8,128)S(1)} %get-tuple-element.15), channel_id=1, source_target_pairs={{0,1},{1,2},{2,3},{3,4},{4,5},{5,6},{6,7},{7,8},{8,9},{9,10},{10,1... | collective-permute-start | bytes 737288 | tf_op jit(solution)/shard_map/ppermute | solution.py:34
  79.1 12.3 %collective-permute-start.4 = (f32[6,5,16,128]{3,1,2,0:T(8,128)S(1)}, f32[6,5,16,128]{3,1,2,0:T(8,128)S(1)}, u32[]{:S(2)}, u32[]{:S(2)}) collective-permute-start(f32[6,5,16,128]{3,1,2,0:T(8,128)S(1)} %get-tuple-element.16), channel_id=1, source_target_pairs={{1,0},{2,1},{3,2},{4,3},{5,4},{6,5},{7,6},{8,7},{9,8},{10,9},{11,1... | collective-permute-start | bytes 737288 | tf_op jit(solution)/shard_map/ppermute | solution.py:34
where the time goes:
time: 93.7 us; the launch traced here: 93.2 us
  local copies, waits for them, and re-layouts  32.6 us (35%)
  matrix products  20.3 us (22%)
  starting transfers between devices  16.4 us (18%)
  waiting for transfers between devices  10.6 us (11%)
  other arithmetic  8.29 us (9%)
  between operations  5.04 us (5%)
    dot_general x6, matrix products, patch_scores(): jnp.dot(conv_weight[depth_tap], sliced, preferred_element_type=jnp.float32)  13.4 us
    ppermute x4, starting transfers between devices, from_behind(): lax.ppermute(value, axis, [(source, source + steps) for source in range(l...  10.8 us
    ppermute x4, waiting for transfers between devices, from_behind(): lax.ppermute(value, axis, [(source, source + steps) for source in range(l...  10.6 us
    slice x2, local copies, waits for them, and re-layouts, patch_scores(): sliced = stacked[:, depth_tap:depth_tap + length].reshape(9 * channels, -1)  8.17 us
    unnamed x34, local copies, waits for them, and re-layouts  7.19 us
    dynamic_update_slice x2, local copies, waits for them, and re-layouts, local(): lax.dynamic_update_slice_in_dim(placed_probs, class_probs, patch_start, 1)  6.91 us
    dot_general x2, matrix products, patch_scores(): jnp.einsum('fkc,fcv->fkv', head_weight.astype(jnp.float32), activated.res...  6.31 us
    select_n x1, other arithmetic, patch_scores(): activated = jnp.where(normed > 0, normed, 0.01 * normed)  4.13 us
  transfers between devices with their start and end apart: 6, of which 3 were waited for; matrix products, arithmetic and copies ran while one was open for 6% of the time, Pallas kernels for 0%

commit v1 on v0

v1 whole, which is shorter than its diff:
```python
import functools

import jax
import jax.numpy as jnp
from jax import lax
from jax.experimental import pallas as pl
from jax.experimental.pallas import tpu as pltpu
from jax.sharding import PartitionSpec as P

MARGIN = 2
RIM = 4
PATCH_X = 10
MOST_ACQ = 8
PRIOR = 0.1
EDGE = RIM + 1
BF = jnp.bfloat16
F32 = jnp.float32


def iota(shape, dim):
    return lax.broadcasted_iota(jnp.int32, shape, dim)


def gauss(index, length):
    scaled = (index - (length - 1) / 2.0) / (length / 4.0)
    return jnp.exp(-0.5 * scaled * scaled)


def kernel(
    feat, wts, gain_ref, bias_ref, head_ref, hbias_ref, offs, keep_ref, acq,
    out,
    before, after, xs, wcat, conv, wpad, snd_lo, snd_hi, rcv_below, rcv_above,
    stat, coef, halo_send, halo_recv, edge_send, edge_recv,
):
    channels, planes, rows, cols = feat.shape
    folds, classes, _ = head_ref.shape
    patches = offs.shape[1]
    prow = rows // patches
    wide = folds * channels
    half = channels // 2
    slabs = lax.axis_size("slab")
    me = lax.axis_index("slab")
    has_left, has_right = me > 0, me < slabs - 1
    left, right = {"slab": me - 1}, {"slab": me + 1}

    barrier = pltpu.get_barrier_semaphore()

    @pl.when(has_left)
    def _():
        pl.semaphore_signal(barrier, inc=1, device_id=left)

    @pl.when(has_right)
    def _():
        pl.semaphore_signal(barrier, inc=1, device_id=right)

    interior = has_left & has_right

    @pl.when(interior)
    def _():
        pl.semaphore_wait(barrier, 2)

    @pl.when(jnp.logical_not(interior))
    def _():
        pl.semaphore_wait(barrier, 1)

    def remote(src, dst, sems, slot, target):
        return pltpu.make_async_remote_copy(
            src_ref=src, dst_ref=dst, send_sem=sems[0].at[slot], recv_sem=sems[1].at[slot],
            device_id=target,
        )

    halo = (halo_send, halo_recv)
    edge = (edge_send, edge_recv)
    halo_right = remote(feat.at[:, planes - RIM :], before, halo, 0, right)
    halo_left = remote(feat.at[:, :RIM], after, halo, 1, left)

    @pl.when(has_right)
    def _():
        halo_right.start()

    @pl.when(has_left)
    def _():
        halo_left.start()

    @pl.when(me == 0)
    def _():
        before[...] = jnp.zeros_like(before)
        rcv_below[...] = jnp.zeros_like(rcv_below)

    @pl.when(me == slabs - 1)
    def _():
        after[...] = jnp.zeros_like(after)
        rcv_above[...] = jnp.zeros_like(rcv_above)

    depth = wts.shape[2]
    for a in range(3):
        wcat[:, a * depth : (a + 1) * depth] = wts[a]
    eye = iota((channels, channels), 0) == iota((channels, channels), 1)

    def column(values):
        return jnp.concatenate(
            [
                jnp.sum(jnp.where(eye, values[f : f + 1, :], 0.0), axis=1, keepdims=True)
                for f in range(folds)
            ],
            axis=0,
        )

    gain_col = column(gain_ref[...])
    bias_col = column(bias_ref[...])
    heads = folds * classes
    head_row = iota((heads, wide), 0)
    head_lane = iota((heads, wide), 1)
    head = jnp.zeros((heads, wide), F32)
    for f in range(folds):
        tiled = jnp.concatenate([head_ref[f].astype(F32)] * folds, axis=1)
        for k in range(classes):
            here = (head_row == k * folds + f) & (head_lane // channels == f)
            head = jnp.where(here, tiled[k : k + 1, :], head)
    head2 = jnp.concatenate([head, head], axis=1).astype(BF)
    hb = jnp.concatenate([hbias_ref[...]] * classes, axis=0)
    pick = iota((heads, classes), 0) // folds == iota((heads, classes), 1)
    head_bias = jnp.sum(jnp.where(pick, hb, 0.0), axis=1, keepdims=True)

    m_i, k_i = iota((half * rows, half * rows), 0), iota((half * rows, half * rows), 1)
    swap = (k_i == (m_i % half) * rows + m_i // half).astype(F32).astype(BF)
    stack = heads * prow
    m_i, k_i = iota((classes * prow, stack), 0), iota((classes * prow, stack), 1)
    gather = (k_i // heads == m_i % prow) & ((k_i % heads) // folds == m_i // prow)
    gather = gather.astype(F32)
    gather = jnp.concatenate([gather, gather], axis=1).astype(BF)

    starts = [RIM - MARGIN + offs[0, p] for p in range(patches)]
    lane = iota((half * rows, cols), 1)
    unit = 3 * channels
    zero_row = jnp.zeros((unit, cols), BF)

    def lay_planes(source, first, base, count, masked):
        @pl.loop(0, count // 2)
        def _(pair):
            pair_planes = [source[:, first + 2 * pair + e].reshape(channels * rows, cols) for e in range(2)]
            for g in range(2):
                part = jnp.concatenate(
                    [v[g * half * rows : (g + 1) * half * rows] for v in pair_planes], axis=1
                )
                turned = jnp.dot(swap, part, preferred_element_type=F32)
                for e in range(2):
                    j = base + 2 * pair + e
                    here = turned[:, e * cols : (e + 1) * cols]
                    taps = (
                        jnp.where(lane == 0, 0.0, pltpu.roll(here, 1, 1)),
                        here,
                        jnp.where(lane == cols - 1, 0.0, pltpu.roll(here, cols - 1, 1)),
                    )
                    for p in range(patches):
                        if masked:
                            inside = (j >= starts[p]) & (j < starts[p] + PATCH_X)
                            factor = jnp.where(inside, 1.0, 0.0)
                        for c, tap in enumerate(taps):
                            mine = tap[p * prow * half : (p + 1) * prow * half]
                            if masked:
                                mine = mine * factor
                            mine = mine.astype(BF)
                            for r in range(prow):
                                at = (r + 1) * unit + c * channels + g * half
                                xs[p, j + 1, at : at + half, :] = mine[r * half : (r + 1) * half]

    span = planes + 2 * RIM
    for p in range(patches):
        xs[p, 0] = jnp.zeros((xs.shape[2], cols), BF)
        xs[p, span + 1] = jnp.zeros((xs.shape[2], cols), BF)

        @pl.loop(1, span + 1)
        def _(j, p=p):
            xs[p, j, 0:unit, :] = zero_row
            xs[p, j, (prow + 1) * unit : (prow + 2) * unit, :] = zero_row

        for j in (*range(RIM), *range(RIM + PATCH_X, 2 * RIM + PATCH_X)):
            wpad[p, j] = jnp.zeros(wpad.shape[2:], F32)

    lay_planes(feat, 0, RIM, planes, False)

    @pl.when(has_left)
    def _():
        remote(feat.at[:, planes - RIM :], before, halo, 0, left).wait_recv()

    @pl.when(has_right)
    def _():
        remote(feat.at[:, :RIM], after, halo, 1, right).wait_recv()

    lay_planes(before, 0, 0, RIM, True)
    lay_planes(after, 0, RIM + planes, RIM, True)

    def conv_plane(p, i):
        x = starts[p] + i
        for pair in range(prow // 2):
            sides = []
            for h in (2 * pair, 2 * pair + 1):
                sides.append(
                    jnp.concatenate(
                        [xs[p, x + a, h * unit : h * unit + depth, :] for a in range(3)], axis=0
                    )
                )
            conv[p, i, :, 2 * pair * cols : (2 * pair + 2) * cols] = jnp.dot(
                wcat[...], jnp.concatenate(sides, axis=1), preferred_element_type=F32
            )

    def shift_of(p):
        total = conv[p, 0, :, 0:cols]
        for h in range(1, prow):
            total = total + conv[p, 0, :, h * cols : (h + 1) * cols]
        mean = jnp.sum(total, axis=1, keepdims=True) * (1.0 / (prow * cols))
        stat[p, 0] = jnp.broadcast_to(mean, (wide, cols))
        stat[p, 1] = jnp.zeros((wide, cols), F32)
        stat[p, 2] = jnp.zeros((wide, cols), F32)

    def add_stats(p, i):
        for lo in range(0, wide, 32):
            rows_here = slice(lo, lo + 32)
            base = stat[p, 0, rows_here]
            first, second = stat[p, 1, rows_here], stat[p, 2, rows_here]
            for h in range(prow):
                d = conv[p, i, rows_here, h * cols : (h + 1) * cols] - base
                first = first + d
                second = second + d * d
            stat[p, 1, rows_here] = first
            stat[p, 2, rows_here] = second

    def affine(p):
        size = 1.0 / (PATCH_X * prow * cols)
        d_mean = jnp.sum(stat[p, 1], axis=1, keepdims=True) * size
        var = jnp.sum(stat[p, 2], axis=1, keepdims=True) * size - d_mean * d_mean
        scale = lax.rsqrt(jnp.maximum(var, 0.0) + 1e-05) * gain_col
        mean = stat[p, 0][:, 0:1] + d_mean
        return scale, bias_col - mean * scale

    row_f = iota((prow, cols), 0).astype(F32)
    col_f = iota((prow, cols), 1).astype(F32)
    flat = gauss(row_f, prow) * gauss(col_f, cols)

    def score_plane(p, i, scale, offset):
        blocks = []
        for pair in range(prow // 2):
            y = conv[p, i, :, 2 * pair * cols : (2 * pair + 2) * cols] * scale + offset
            y = jnp.maximum(y, 0.01 * y)
            big = y.astype(BF)
            small = (y - big.astype(F32)).astype(BF)
            logits = jnp.dot(
                head2, jnp.concatenate([big, small], axis=0), preferred_element_type=F32
            ) + head_bias
            groups = [logits[j : j + 8] for j in range(0, heads, 8)]
            top = functools.reduce(jnp.maximum, groups)
            top = jnp.maximum(top, pltpu.roll(top, 4, 0))
            exps = [jnp.exp(v - top) for v in groups]
            total = functools.reduce(jnp.add, exps)
            total = total + pltpu.roll(total, 4, 0)
            inverse = 1.0 / total
            probs = jnp.concatenate([v * inverse for v in exps], axis=0)
            blocks += [probs[:, :cols], probs[:, cols:]]
        tall = jnp.concatenate(blocks, axis=0)
        big = tall.astype(BF)
        small = (tall - big.astype(F32)).astype(BF)
        summed = jnp.dot(
            gather, jnp.concatenate([big, small], axis=0), preferred_element_type=F32
        )
        index = lax.convert_element_type(i, F32)
        keep = keep_ref[0, p].astype(F32)
        window = gauss(jnp.full((prow, cols), index, F32), PATCH_X) * flat * keep
        share = window * (1.0 / folds)
        for k in range(classes):
            wpad[p, RIM + i, k] = summed[k * prow : (k + 1) * prow] * share
        wpad[p, RIM + i, classes] = window

    def send_edges(p):
        for j in range(EDGE):
            snd_lo[p, j] = wpad[p, j - starts[p] + RIM]
            snd_hi[p, j] = wpad[p, RIM + planes - 1 + j - starts[p] + RIM]

        @pl.when(has_right)
        def _():
            remote(snd_hi.at[p], rcv_below.at[p], edge, 2 * p, right).start()

        @pl.when(has_left)
        def _():
            remote(snd_lo.at[p], rcv_above.at[p], edge, 2 * p + 1, left).start()

    conv_plane(0, 0)
    shift_of(0)
    add_stats(0, 0)

    @pl.loop(1, PATCH_X)
    def _(i):
        conv_plane(0, i)
        add_stats(0, i)

    for p in range(patches):
        scale, offset = affine(p)
        if p + 1 < patches:
            conv_plane(p + 1, 0)
            shift_of(p + 1)
            add_stats(p + 1, 0)
            score_plane(p, 0, scale, offset)

            @pl.loop(1, PATCH_X)
            def _(i, p=p, scale=scale, offset=offset):
                conv_plane(p + 1, i)
                score_plane(p, i, scale, offset)
                add_stats(p + 1, i)
        else:

            @pl.loop(0, PATCH_X)
            def _(i, p=p, scale=scale, offset=offset):
                score_plane(p, i, scale, offset)

        send_edges(p)

    shape = (prow, cols)
    count = jnp.full(shape, acq[0].astype(F32), F32)
    step = planes / jnp.maximum(count - 1.0, 1.0)
    anchor = jnp.full(shape, (me * planes).astype(F32), F32)
    last = (slabs * planes - 1) * 1.0
    for slot in range(MOST_ACQ):
        position = jnp.clip(anchor + (slot * step - 0.5), 0.0, last) - anchor
        for e in range(planes + 2):
            value = jnp.maximum(0.0, 1.0 - jnp.abs(position - (e - 1.0)))
            coef[slot, e] = jnp.where(count > slot, value, 0.0)

    for p in range(patches):

        @pl.when(has_right)
        def _():
            remote(snd_hi.at[p], rcv_below.at[p], edge, 2 * p, right).wait_send()
            remote(snd_lo.at[p], rcv_above.at[p], edge, 2 * p + 1, right).wait_recv()

        @pl.when(has_left)
        def _():
            remote(snd_lo.at[p], rcv_above.at[p], edge, 2 * p + 1, left).wait_send()
            remote(snd_hi.at[p], rcv_below.at[p], edge, 2 * p, left).wait_recv()

        def total(e, k):
            value = wpad[p, e + RIM - 1 - starts[p] + RIM, k]
            if e < EDGE:
                value = value + rcv_below[p, e, k]
            if e >= planes + 2 - EDGE:
                value = value + rcv_above[p, e - (planes + 2 - EDGE), k]
            return value

        inverses = [1.0 / (total(e, classes) + PRIOR) for e in range(planes + 2)]
        for k in range(classes):
            merged = []
            for e in range(planes + 2):
                value = total(e, k)
                if k == 0:
                    value = value + PRIOR
                merged.append(value * inverses[e])
            for slot in range(MOST_ACQ):
                value = coef[slot, 0] * merged[0]
                for e in range(1, planes + 2):
                    value = value + coef[slot, e] * merged[e]
                out[k, slot, p * prow : (p + 1) * prow, :] = value

    @pl.when(has_right)
    def _():
        halo_right.wait_send()

    @pl.when(has_left)
    def _():
        halo_left.wait_send()


def local(features, conv_weight, norm_gain, norm_bias, head_weight, head_bias, patch_offsets, fg_mask, acq_counts):
    channels, planes, rows, cols = features.shape
    folds, classes, _ = head_weight.shape
    patches = patch_offsets.shape[1]
    prow = rows // patches
    wide = folds * channels
    span = planes + 2 * RIM
    vmem = pl.BlockSpec(memory_space=pltpu.VMEM)
    smem = pl.BlockSpec(memory_space=pltpu.SMEM)
    edges = pltpu.VMEM((patches, EDGE, classes + 1, prow, cols), F32)
    cells = PATCH_X * prow * cols * patches
    return pl.pallas_call(
        kernel,
        out_shape=jax.ShapeDtypeStruct((classes, MOST_ACQ, rows, cols), F32),
        in_specs=[vmem] * 6 + [smem] * 3,
        out_specs=vmem,
        scratch_shapes=[
            pltpu.VMEM((channels, RIM, rows, cols), BF),
            pltpu.VMEM((channels, RIM, rows, cols), BF),
            pltpu.VMEM((patches, span + 2, (prow + 2) * 3 * channels, cols), BF),
            pltpu.VMEM((wide, 27 * channels), BF),
            pltpu.VMEM((patches, PATCH_X, wide, prow * cols), F32),
            pltpu.VMEM((patches, PATCH_X + 2 * RIM, classes + 1, prow, cols), F32),
            edges, edges, edges, edges,
            pltpu.VMEM((patches, 3, wide, cols), F32),
            pltpu.VMEM((MOST_ACQ, planes + 2, prow, cols), F32),
            pltpu.SemaphoreType.DMA((2,)),
            pltpu.SemaphoreType.DMA((2,)),
            pltpu.SemaphoreType.DMA((2 * patches,)),
            pltpu.SemaphoreType.DMA((2 * patches,)),
        ],
        compiler_params=pltpu.CompilerParams(
            collective_id=0, has_side_effects=True, vmem_limit_bytes=56 * 1024 * 1024
        ),
        cost_estimate=pl.CostEstimate(
            flops=2 * cells * wide * 27 * channels,
            bytes_accessed=2 * features.size + 4 * classes * MOST_ACQ * rows * cols,
            transcendentals=cells * folds * classes,
        ),
    )(features, conv_weight, norm_gain, norm_bias, head_weight, head_bias, patch_offsets, fg_mask, acq_counts)


def solution(mesh):
    whole = P(None, ("brain", "slab"), None, None)
    by_slab = P(("brain", "slab"), None)
    in_specs = (whole, P(), P(), P(), P(), P(), by_slab, by_slab, P(("brain", "slab")))
    return jax.shard_map(local, mesh=mesh, in_specs=in_specs, out_specs=whole, check_vma=False)
```

time: 93.7 us -> 46.4 us (0.50)
  the two profiles are of different devices: /device:TPU:11 before, /device:TPU:1 now
where the time goes in v1:
time: 46.4 us; the launch traced here: 46.1 us
  Pallas kernels  40.6 us (88%)
  local copies, waits for them, and re-layouts  4.89 us (11%)
  between operations  0.66 us (1%)
    pallas_call x1, Pallas kernels, local(): pl.pallas_call(kernel, out_shape=jax.ShapeDtypeStruct((classes, MOST_ACQ,...  40.6 us
    unnamed x3, local copies, waits for them, and re-layouts  4.89 us

profile of v1, /device:TPU:1, one launch (start us, length us, event | category | flops | bytes accessed | tf_op | source)
XLA Modules:
  0.0 46.1 jit_solution(6601349681227980369)
XLA Ops:
  0.7 1.3 %copy.11.head_ref = bf16[4,6,32]{2,1,0:T(8,128)(2,1)} copy(bf16[4,6,32]{2,0,1:T(4,128)(2,1)} %param.13) | data formatting | bytes 3072 | tf_op args[4]
  1.9 1.8 %copy.10.wts = bf16[3,128,288]{2,1,0:T(8,128)(2,1)} copy(bf16[3,128,288]{1,2,0:T(8,128)(2,1)} %param.10) | data formatting | bytes 442368 | tf_op args[1]
  3.8 40.6 %shard_map.91 = f32[6,8,16,128]{3,2,1,0:T(8,128)} custom-call(bf16[32,6,16,128]{3,2,1,0:T(8,128)(2,1)} %feat.1, bf16[3,128,288]{2,1,0:T(8,128)(2,1)} %copy.10.wts, f32[4,32]{1,0:T(4,128)} %gain_ref.1, f32[4,32]{1,0:T(4,128)} %bias_ref.1, bf16[4,6,32]{2,1,0:T(8,128)(2,1)} %copy.11.head_ref, f32[4,6]{1,0:T(4,128)} %hbias_ref.1, s32[1,2]{1,0:T(1,128)} %offs.1, ...), custom_call_target="tpu_custom_call" | custom-call | flops 4529848320 | bytes 1179648 | tf_op jit(solution)/shard_map/pallas_call | solution.py:382
  44.3 1.8 %copy.14 = f32[6,8,16,128]{3,2,1,0:T(8,128)} copy(f32[6,8,16,128]{3,2,1,0:T(8,128)} %shard_map.91) | data formatting | bytes 786432

commit v2 on v1

--- a/solution.py
+++ b/solution.py
@@ -33,7 +33,7 @@
     stat, coef, halo_send, halo_recv, edge_send, edge_recv,
 ):
     channels, planes, rows, cols = feat.shape
-    folds, classes, _ = head_ref.shape
+    classes, folds, _ = head_ref.shape
     patches = offs.shape[1]
     prow = rows // patches
     wide = folds * channels
@@ -92,9 +92,11 @@
         after[...] = jnp.zeros_like(after)
         rcv_above[...] = jnp.zeros_like(rcv_above)
 
-    depth = wts.shape[2]
-    for a in range(3):
-        wcat[:, a * depth : (a + 1) * depth] = wts[a]
+    depth = wts.shape[1]
+    same = (iota((wide, wide), 0) == iota((wide, wide), 1)).astype(F32).astype(BF)
+    wcat[...] = lax.dot_general(
+        same, wts[...].reshape(3 * depth, wide), (((1,), (1,)), ((), ())), preferred_element_type=F32
+    ).astype(BF)
     eye = iota((channels, channels), 0) == iota((channels, channels), 1)
 
     def column(values):
@@ -111,12 +113,9 @@
     heads = folds * classes
     head_row = iota((heads, wide), 0)
     head_lane = iota((heads, wide), 1)
-    head = jnp.zeros((heads, wide), F32)
-    for f in range(folds):
-        tiled = jnp.concatenate([head_ref[f].astype(F32)] * folds, axis=1)
-        for k in range(classes):
-            here = (head_row == k * folds + f) & (head_lane // channels == f)
-            head = jnp.where(here, tiled[k : k + 1, :], head)
+    flat_head = head_ref[...].astype(F32).reshape(heads, channels)
+    head = jnp.concatenate([flat_head] * folds, axis=1)
+    head = jnp.where(head_lane // channels == head_row % folds, head, 0.0)
     head2 = jnp.concatenate([head, head], axis=1).astype(BF)
     hb = jnp.concatenate([hbias_ref[...]] * classes, axis=0)
     pick = iota((heads, classes), 0) // folds == iota((heads, classes), 1)
@@ -175,24 +174,17 @@
             xs[p, j, 0:unit, :] = zero_row
             xs[p, j, (prow + 1) * unit : (prow + 2) * unit, :] = zero_row
 
-        for j in (*range(RIM), *range(RIM + PATCH_X, 2 * RIM + PATCH_X)):
-            wpad[p, j] = jnp.zeros(wpad.shape[2:], F32)
+        wpad[p, PATCH_X] = jnp.zeros(wpad.shape[2:], F32)
 
     lay_planes(feat, 0, RIM, planes, False)
 
-    @pl.when(has_left)
-    def _():
-        remote(feat.at[:, planes - RIM :], before, halo, 0, left).wait_recv()
-
-    @pl.when(has_right)
-    def _():
-        remote(feat.at[:, :RIM], after, halo, 1, right).wait_recv()
-
-    lay_planes(before, 0, 0, RIM, True)
-    lay_planes(after, 0, RIM + planes, RIM, True)
-
-    def conv_plane(p, i):
-        x = starts[p] + i
+    inner = planes - 2
+    rest = PATCH_X - inner
+
+    def rest_index(p, t):
+        return t + jnp.where(starts[p] + t <= RIM, 0, inner)
+
+    def conv_plane(p, i, x):
         for pair in range(prow // 2):
             sides = []
             for h in (2 * pair, 2 * pair + 1):
@@ -238,7 +230,7 @@
     col_f = iota((prow, cols), 1).astype(F32)
     flat = gauss(row_f, prow) * gauss(col_f, cols)
 
-    def score_plane(p, i, scale, offset):
+    def score_plane(p, i, index, scale, offset):
         blocks = []
         for pair in range(prow // 2):
             y = conv[p, i, :, 2 * pair * cols : (2 * pair + 2) * cols] * scale + offset
@@ -263,18 +255,26 @@
         summed = jnp.dot(
             gather, jnp.concatenate([big, small], axis=0), preferred_element_type=F32
         )
-        index = lax.convert_element_type(i, F32)
+        index = lax.convert_element_type(index, F32)
         keep = keep_ref[0, p].astype(F32)
         window = gauss(jnp.full((prow, cols), index, F32), PATCH_X) * flat * keep
         share = window * (1.0 / folds)
         for k in range(classes):
-            wpad[p, RIM + i, k] = summed[k * prow : (k + 1) * prow] * share
-        wpad[p, RIM + i, classes] = window
+            wpad[p, i, k] = summed[k * prow : (k + 1) * prow] * share
+        wpad[p, i, classes] = window
+
+    def slot_of(p, j):
+        if RIM < j < RIM + planes - 1:
+            return j - RIM - 1
+        i = j - starts[p]
+        if j <= RIM:
+            return jnp.where(i >= 0, inner + i, PATCH_X)
+        return jnp.where(i < PATCH_X, i, PATCH_X)
 
     def send_edges(p):
         for j in range(EDGE):
-            snd_lo[p, j] = wpad[p, j - starts[p] + RIM]
-            snd_hi[p, j] = wpad[p, RIM + planes - 1 + j - starts[p] + RIM]
+            snd_lo[p, j] = wpad[p, slot_of(p, j)]
+            snd_hi[p, j] = wpad[p, slot_of(p, RIM + planes - 1 + j)]
 
         @pl.when(has_right)
         def _():
@@ -284,35 +284,54 @@
         def _():
             remote(snd_lo.at[p], rcv_above.at[p], edge, 2 * p + 1, left).start()
 
-    conv_plane(0, 0)
-    shift_of(0)
-    add_stats(0, 0)
-
-    @pl.loop(1, PATCH_X)
+    for p in range(patches):
+        conv_plane(p, 0, RIM + 1)
+        shift_of(p)
+        add_stats(p, 0)
+
+        @pl.loop(1, inner)
+        def _(i, p=p):
+            conv_plane(p, i, RIM + 1 + i)
+            add_stats(p, i)
+
+    @pl.when(has_left)
+    def _():
+        remote(feat.at[:, planes - RIM :], before, halo, 0, left).wait_recv()
+
+    @pl.when(has_right)
+    def _():
+        remote(feat.at[:, :RIM], after, halo, 1, right).wait_recv()
+
+    lay_planes(before, 0, 0, RIM, True)
+    lay_planes(after, 0, RIM + planes, RIM, True)
+
+    def conv_rest(p, t):
+        conv_plane(p, inner + t, starts[p] + rest_index(p, t))
+        add_stats(p, inner + t)
+
+    def score_rest(p, t, norms):
+        score_plane(p, inner + t, rest_index(p, t), *norms)
+
+    @pl.loop(0, rest)
+    def _(t):
+        conv_rest(0, t)
+
+    norms = []
+    for p in range(patches):
+        norms.append(affine(p))
+
+        @pl.loop(0, rest)
+        def _(t, p=p):
+            if p + 1 < patches:
+                conv_rest(p + 1, t)
+            score_rest(p, t, norms[p])
+
+        send_edges(p)
+
+    @pl.loop(0, inner)
     def _(i):
-        conv_plane(0, i)
-        add_stats(0, i)
-
-    for p in range(patches):
-        scale, offset = affine(p)
-        if p + 1 < patches:
-            conv_plane(p + 1, 0)
-            shift_of(p + 1)
-            add_stats(p + 1, 0)
-            score_plane(p, 0, scale, offset)
-
-            @pl.loop(1, PATCH_X)
-            def _(i, p=p, scale=scale, offset=offset):
-                conv_plane(p + 1, i)
-                score_plane(p, i, scale, offset)
-                add_stats(p + 1, i)
-        else:
-
-            @pl.loop(0, PATCH_X)
-            def _(i, p=p, scale=scale, offset=offset):
-                score_plane(p, i, scale, offset)
-
-        send_edges(p)
+        for p in range(patches):
+            score_plane(p, i, RIM + 1 + i - starts[p], *norms[p])
 
     shape = (prow, cols)
     count = jnp.full(shape, acq[0].astype(F32), F32)
@@ -338,7 +357,7 @@
             remote(snd_hi.at[p], rcv_below.at[p], edge, 2 * p, left).wait_recv()
 
         def total(e, k):
-            value = wpad[p, e + RIM - 1 - starts[p] + RIM, k]
+            value = wpad[p, slot_of(p, e + RIM - 1), k]
             if e < EDGE:
                 value = value + rcv_below[p, e, k]
             if e >= planes + 2 - EDGE:
@@ -390,7 +409,7 @@
             pltpu.VMEM((patches, span + 2, (prow + 2) * 3 * channels, cols), BF),
             pltpu.VMEM((wide, 27 * channels), BF),
             pltpu.VMEM((patches, PATCH_X, wide, prow * cols), F32),
-            pltpu.VMEM((patches, PATCH_X + 2 * RIM, classes + 1, prow, cols), F32),
+            pltpu.VMEM((patches, PATCH_X + 1, classes + 1, prow, cols), F32),
             edges, edges, edges, edges,
             pltpu.VMEM((patches, 3, wide, cols), F32),
             pltpu.VMEM((MOST_ACQ, planes + 2, prow, cols), F32),
@@ -400,14 +419,14 @@
             pltpu.SemaphoreType.DMA((2 * patches,)),
         ],
         compiler_params=pltpu.CompilerParams(
-            collective_id=0, has_side_effects=True, vmem_limit_bytes=56 * 1024 * 1024
+            collective_id=0, has_side_effects=True, vmem_limit_bytes=30 * 1024 * 1024
         ),
         cost_estimate=pl.CostEstimate(
             flops=2 * cells * wide * 27 * channels,
             bytes_accessed=2 * features.size + 4 * classes * MOST_ACQ * rows * cols,
             transcendentals=cells * folds * classes,
         ),
-    )(features, conv_weight, norm_gain, norm_bias, head_weight, head_bias, patch_offsets, fg_mask, acq_counts)
+    )(features, jnp.swapaxes(conv_weight, 1, 2), norm_gain, norm_bias, jnp.swapaxes(head_weight, 0, 1), head_bias, patch_offsets, fg_mask, acq_counts)
 
 
 def solution(mesh):

time: 46.4 us -> 38.4 us (0.83)
  Pallas kernels: 40.6 us -> 32.5 us
    pallas_call x1, Pallas kernels: 40.6 us -> 32.5 us  [local(): pl.pallas_call(kernel, out_shape=jax.ShapeDtypeStruct((classes, MOST_ACQ,...]
    unnamed x3 -> x17, local copies, waits for them, and re-layouts: 4.89 us -> 4.85 us
where the time goes in v2:
time: 38.4 us; the launch traced here: 38.1 us
  Pallas kernels  32.5 us (85%)
  local copies, waits for them, and re-layouts  4.85 us (13%)
  between operations  0.71 us (2%)
    pallas_call x1, Pallas kernels, local(): pl.pallas_call(kernel, out_shape=jax.ShapeDtypeStruct((classes, MOST_ACQ,...  32.5 us
    unnamed x17, local copies, waits for them, and re-layouts  4.85 us

profile of v2, /device:TPU:1, one launch (start us, length us, event | category | flops | bytes accessed | tf_op | source)
XLA Modules:
  0.0 38.1 jit_solution(12259998611864720939)
XLA Ops:
  0.0 0.0 copy-start.4
  0.7 0.0 copy-start.3
  0.7 0.0 copy-start.6
  0.7 0.0 copy-start.7
  0.7 0.0 copy-done.4
  0.7 0.6 %copy-done.3 = f32[4,32]{1,0:T(4,128)S(1)} copy-done((f32[4,32]{1,0:T(4,128)S(1)}, f32[4,32]{1,0:T(4,128)}, u32[]{:S(2)}) %copy-start.3) | copy-done | bytes 536
  1.4 0.0 copy-done.6
  1.4 0.0 copy-done.7
  1.4 0.0 copy-start
  1.4 1.1 %copy-done = bf16[32,6,16,128]{3,2,1,0:T(8,128)(2,1)S(1)} copy-done((bf16[32,6,16,128]{3,2,1,0:T(8,128)(2,1)S(1)}, bf16[32,6,16,128]{3,2,1,0:T(8,128)(2,1)}, u32[]{:S(2)}) %copy-start) | copy-done | bytes 786456
  2.5 0.0 copy-start.1
  2.5 0.9 %copy-done.1 = bf16[3,128,288]{1,2,0:T(8,128)(2,1)S(1)} copy-done((bf16[3,128,288]{1,2,0:T(8,128)(2,1)S(1)}, bf16[3,128,288]{1,2,0:T(8,128)(2,1)}, u32[]{:S(2)}) %copy-start.1) | copy-done | bytes 221208
  3.4 0.0 copy-start.2
  3.4 0.7 %copy-done.2 = bf16[4,6,32]{2,0,1:T(4,128)(2,1)S(1)} copy-done((bf16[4,6,32]{2,0,1:T(4,128)(2,1)S(1)}, bf16[4,6,32]{2,0,1:T(4,128)(2,1)}, u32[]{:S(2)}) %copy-start.2) | copy-done | bytes 1560
  4.1 0.0 copy-start.5
  4.1 0.7 %copy-done.5 = f32[4,6]{1,0:T(4,128)S(1)} copy-done((f32[4,6]{1,0:T(4,128)S(1)}, f32[4,6]{1,0:T(4,128)}, u32[]{:S(2)}) %copy-start.5) | copy-done | bytes 120
  4.8 32.5 %shard_map.91 = f32[6,8,16,128]{3,2,1,0:T(8,128)S(1)} custom-call(bf16[32,6,16,128]{3,2,1,0:T(8,128)(2,1)S(1)} %copy-done, bf16[3,288,128]{2,1,0:T(8,128)(2,1)S(1)} %bitcast.2, f32[4,32]{1,0:T(4,128)S(1)} %copy-done.3, f32[4,32]{1,0:T(4,128)S(1)} %copy-done.4, bf16[6,4,32]{2,1,0:T(4,128)(2,1)S(1)} %bitcast.3, f32[4,6]{1,0:T(4,128)S(1)} %copy-done.5, ...), custom_call_target="tpu_custom_call" | custom-call | flops 4529848320 | bytes 1179648 | tf_op jit(solution)/shard_map/pallas_call | solution.py:401
  37.3 0.7 %copy.12 = f32[6,8,16,128]{3,2,1,0:T(8,128)} copy(f32[6,8,16,128]{3,2,1,0:T(8,128)S(1)} %shard_map.91) | data formatting | bytes 786432
Async XLA Ops:
  0.0 0.7 %copy-start.4 = (f32[4,32]{1,0:T(4,128)S(1)}, f32[4,32]{1,0:T(4,128)}, u32[]{:S(2)}) copy-start(f32[4,32]{1,0:T(4,128)} %bias_ref.1) | copy-start | bytes 1540
  0.7 0.7 %copy-start.3 = (f32[4,32]{1,0:T(4,128)S(1)}, f32[4,32]{1,0:T(4,128)}, u32[]{:S(2)}) copy-start(f32[4,32]{1,0:T(4,128)} %gain_ref.1) | copy-start | bytes 1540
  0.7 0.7 %copy-start.6 = (s32[1,2]{1,0:T(1,128)S(1)}, s32[1,2]{1,0:T(1,128)}, u32[]{:S(2)}) copy-start(s32[1,2]{1,0:T(1,128)} %offs.1) | copy-start | bytes 28
  0.7 0.7 %copy-start.7 = (s32[1,2]{1,0:T(1,128)S(1)}, s32[1,2]{1,0:T(1,128)}, u32[]{:S(2)}) copy-start(s32[1,2]{1,0:T(1,128)} %keep_ref.1) | copy-start | bytes 28
  1.4 1.1 %copy-start = (bf16[32,6,16,128]{3,2,1,0:T(8,128)(2,1)S(1)}, bf16[32,6,16,128]{3,2,1,0:T(8,128)(2,1)}, u32[]{:S(2)}) copy-start(bf16[32,6,16,128]{3,2,1,0:T(8,128)(2,1)} %feat.1) | copy-start | bytes 2359300
  2.5 0.9 %copy-start.1 = (bf16[3,128,288]{1,2,0:T(8,128)(2,1)S(1)}, bf16[3,128,288]{1,2,0:T(8,128)(2,1)}, u32[]{:S(2)}) copy-start(bf16[3,128,288]{1,2,0:T(8,128)(2,1)} %param.10) | copy-start | bytes 663556
  3.4 0.7 %copy-start.2 = (bf16[4,6,32]{2,0,1:T(4,128)(2,1)S(1)}, bf16[4,6,32]{2,0,1:T(4,128)(2,1)}, u32[]{:S(2)}) copy-start(bf16[4,6,32]{2,0,1:T(4,128)(2,1)} %param.13) | copy-start | bytes 4612
  4.1 0.7 %copy-start.5 = (f32[4,6]{1,0:T(4,128)S(1)}, f32[4,6]{1,0:T(4,128)}, u32[]{:S(2)}) copy-start(f32[4,6]{1,0:T(4,128)} %hbias_ref.1) | copy-start | bytes 292

commit v3 on v2

--- a/solution.py
+++ b/solution.py
@@ -12,6 +12,7 @@
 PATCH_X = 10
 MOST_ACQ = 8
 PRIOR = 0.1
+LEVELS = 65000
 EDGE = RIM + 1
 BF = jnp.bfloat16
 F32 = jnp.float32
@@ -27,10 +28,12 @@
 
 
 def kernel(
-    feat, wts, gain_ref, bias_ref, head_ref, hbias_ref, offs, keep_ref, acq,
+    feat_in, wts_in, gain_in, bias_in, head_in, hbias_in, offs, keep_ref, acq,
     out,
-    before, after, xs, wcat, conv, wpad, snd_lo, snd_hi, rcv_below, rcv_above,
-    stat, coef, halo_send, halo_recv, edge_send, edge_recv,
+    feat, wts, gain_ref, bias_ref, head_ref, hbias_ref,
+    before, after, xs, wcat, conv, wpad, codes, snd_lo, snd_hi, rcv_below, rcv_above,
+    meta_lo, meta_hi, meta_below, meta_above,
+    stat, coef, load_sems, halo_send, halo_recv, edge_send, edge_recv,
 ):
     channels, planes, rows, cols = feat.shape
     classes, folds, _ = head_ref.shape
@@ -43,6 +46,18 @@
     has_left, has_right = me > 0, me < slabs - 1
     left, right = {"slab": me - 1}, {"slab": me + 1}
 
+    loads = [
+        pltpu.make_async_copy(src, dst, load_sems.at[i])
+        for i, (src, dst) in enumerate(
+            (
+                (feat_in, feat), (wts_in, wts), (gain_in, gain_ref), (bias_in, bias_ref),
+                (head_in, head_ref), (hbias_in, hbias_ref),
+            )
+        )
+    ]
+    for load in loads:
+        load.start()
+
     barrier = pltpu.get_barrier_semaphore()
 
     @pl.when(has_left)
@@ -71,26 +86,47 @@
 
     halo = (halo_send, halo_recv)
     edge = (edge_send, edge_recv)
-    halo_right = remote(feat.at[:, planes - RIM :], before, halo, 0, right)
-    halo_left = remote(feat.at[:, :RIM], after, halo, 1, left)
+    halo_right = remote(feat_in.at[:, planes - RIM :], before, halo, 0, right)
+    halo_left = remote(feat_in.at[:, :RIM], after, halo, 1, left)
+
+    meta_right = remote(meta_hi, meta_below, halo, 2, right)
+    meta_left = remote(meta_lo, meta_above, halo, 3, left)
+    starts = [RIM - MARGIN + offs[0, p] for p in range(patches)]
+    for p in range(patches):
+        index = iota((8, cols), 0) - starts[p]
+        keep = keep_ref[0, p].astype(F32)
+        for ref, base in ((meta_lo, 0), (meta_hi, RIM + planes - 1)):
+            i = index + base
+            factor = gauss(i.astype(F32), PATCH_X) * keep
+            ref[p] = jnp.where((i >= 0) & (i < PATCH_X), factor, 0.0)
 
     @pl.when(has_right)
     def _():
         halo_right.start()
+        meta_right.start()
 
     @pl.when(has_left)
     def _():
         halo_left.start()
+        meta_left.start()
 
     @pl.when(me == 0)
     def _():
         before[...] = jnp.zeros_like(before)
         rcv_below[...] = jnp.zeros_like(rcv_below)
+        meta_below[...] = jnp.zeros_like(meta_below)
 
     @pl.when(me == slabs - 1)
     def _():
         after[...] = jnp.zeros_like(after)
         rcv_above[...] = jnp.zeros_like(rcv_above)
+        meta_above[...] = jnp.zeros_like(meta_above)
+
+    for load in loads[1:]:
+        load.wait()
+
+    inner = planes - 2
+    rest = PATCH_X - inner
 
     depth = wts.shape[1]
     same = (iota((wide, wide), 0) == iota((wide, wide), 1)).astype(F32).astype(BF)
@@ -129,7 +165,6 @@
     gather = gather.astype(F32)
     gather = jnp.concatenate([gather, gather], axis=1).astype(BF)
 
-    starts = [RIM - MARGIN + offs[0, p] for p in range(patches)]
     lane = iota((half * rows, cols), 1)
     unit = 3 * channels
     zero_row = jnp.zeros((unit, cols), BF)
@@ -175,11 +210,10 @@
             xs[p, j, (prow + 1) * unit : (prow + 2) * unit, :] = zero_row
 
         wpad[p, PATCH_X] = jnp.zeros(wpad.shape[2:], F32)
-
+        codes[p, rest] = jnp.zeros(codes.shape[2:], codes.dtype)
+
+    loads[0].wait()
     lay_planes(feat, 0, RIM, planes, False)
-
-    inner = planes - 2
-    rest = PATCH_X - inner
 
     def rest_index(p, t):
         return t + jnp.where(starts[p] + t <= RIM, 0, inner)
@@ -230,7 +264,7 @@
     col_f = iota((prow, cols), 1).astype(F32)
     flat = gauss(row_f, prow) * gauss(col_f, cols)
 
-    def score_plane(p, i, index, scale, offset):
+    def score_plane(p, i, index, scale, offset, code=None):
         blocks = []
         for pair in range(prow // 2):
             y = conv[p, i, :, 2 * pair * cols : (2 * pair + 2) * cols] * scale + offset
@@ -262,6 +296,10 @@
         for k in range(classes):
             wpad[p, i, k] = summed[k * prow : (k + 1) * prow] * share
         wpad[p, i, classes] = window
+        if code is not None:
+            coded = (summed * (LEVELS / folds) + 0.5).astype(jnp.int32) - LEVELS // 2
+            for k in range(classes // 2):
+                codes[p, code, k] = coded[2 * k * prow : 2 * (k + 1) * prow].astype(jnp.int16)
 
     def slot_of(p, j):
         if RIM < j < RIM + planes - 1:
@@ -273,8 +311,8 @@
 
     def send_edges(p):
         for j in range(EDGE):
-            snd_lo[p, j] = wpad[p, slot_of(p, j)]
-            snd_hi[p, j] = wpad[p, slot_of(p, RIM + planes - 1 + j)]
+            snd_lo[p, j] = codes[p, slot_of(p, j) - inner]
+            snd_hi[p, j] = codes[p, slot_of(p, RIM + planes - 1 + j) - inner]
 
         @pl.when(has_right)
         def _():
@@ -296,11 +334,13 @@
 
     @pl.when(has_left)
     def _():
-        remote(feat.at[:, planes - RIM :], before, halo, 0, left).wait_recv()
+        remote(feat_in.at[:, planes - RIM :], before, halo, 0, left).wait_recv()
+        remote(meta_hi, meta_below, halo, 2, left).wait_recv()
 
     @pl.when(has_right)
     def _():
-        remote(feat.at[:, :RIM], after, halo, 1, right).wait_recv()
+        remote(feat_in.at[:, :RIM], after, halo, 1, right).wait_recv()
+        remote(meta_lo, meta_above, halo, 3, right).wait_recv()
 
     lay_planes(before, 0, 0, RIM, True)
     lay_planes(after, 0, RIM + planes, RIM, True)
@@ -310,7 +350,7 @@
         add_stats(p, inner + t)
 
     def score_rest(p, t, norms):
-        score_plane(p, inner + t, rest_index(p, t), *norms)
+        score_plane(p, inner + t, rest_index(p, t), *norms, code=t)
 
     @pl.loop(0, rest)
     def _(t):
@@ -356,12 +396,19 @@
             remote(snd_lo.at[p], rcv_above.at[p], edge, 2 * p + 1, left).wait_send()
             remote(snd_hi.at[p], rcv_below.at[p], edge, 2 * p, left).wait_recv()
 
+        ends = [(e, rcv_below, meta_below, e) for e in range(EDGE)]
+        ends += [(planes + 2 - EDGE + j, rcv_above, meta_above, j) for j in range(EDGE)]
+
         def total(e, k):
             value = wpad[p, slot_of(p, e + RIM - 1), k]
-            if e < EDGE:
-                value = value + rcv_below[p, e, k]
-            if e >= planes + 2 - EDGE:
-                value = value + rcv_above[p, e - (planes + 2 - EDGE), k]
+            for plane, codes_in, meta, j in ends:
+                if plane == e:
+                    window = meta[p, j : j + 1, :] * flat
+                    if k < classes:
+                        half_at = (k % 2) * prow
+                        got = codes_in[p, j, k // 2].astype(F32)[half_at : half_at + prow]
+                        window = window * (got * (1.0 / LEVELS) + (LEVELS // 2) / LEVELS)
+                    value = value + window
             return value
 
         inverses = [1.0 / (total(e, classes) + PRIOR) for e in range(planes + 2)]
@@ -381,10 +428,12 @@
     @pl.when(has_right)
     def _():
         halo_right.wait_send()
+        meta_right.wait_send()
 
     @pl.when(has_left)
     def _():
         halo_left.wait_send()
+        meta_left.wait_send()
 
 
 def local(features, conv_weight, norm_gain, norm_bias, head_weight, head_bias, patch_offsets, fg_mask, acq_counts):
@@ -396,37 +445,48 @@
     span = planes + 2 * RIM
     vmem = pl.BlockSpec(memory_space=pltpu.VMEM)
     smem = pl.BlockSpec(memory_space=pltpu.SMEM)
-    edges = pltpu.VMEM((patches, EDGE, classes + 1, prow, cols), F32)
+    hbm = pl.BlockSpec(memory_space=pltpu.MemorySpace.HBM)
+    edges = pltpu.VMEM((patches, EDGE, classes // 2, 2 * prow, cols), jnp.int16)
+    meta = pltpu.VMEM((patches, 8, cols), F32)
+    rest = PATCH_X - (planes - 2)
+    operands = (
+        features, jnp.swapaxes(conv_weight, 1, 2), norm_gain, norm_bias,
+        jnp.swapaxes(head_weight, 0, 1), head_bias,
+    )
     cells = PATCH_X * prow * cols * patches
     return pl.pallas_call(
         kernel,
         out_shape=jax.ShapeDtypeStruct((classes, MOST_ACQ, rows, cols), F32),
-        in_specs=[vmem] * 6 + [smem] * 3,
+        in_specs=[hbm] * 6 + [smem] * 3,
         out_specs=vmem,
         scratch_shapes=[
+            *[pltpu.VMEM(value.shape, value.dtype) for value in operands],
             pltpu.VMEM((channels, RIM, rows, cols), BF),
             pltpu.VMEM((channels, RIM, rows, cols), BF),
             pltpu.VMEM((patches, span + 2, (prow + 2) * 3 * channels, cols), BF),
             pltpu.VMEM((wide, 27 * channels), BF),
             pltpu.VMEM((patches, PATCH_X, wide, prow * cols), F32),
             pltpu.VMEM((patches, PATCH_X + 1, classes + 1, prow, cols), F32),
+            pltpu.VMEM((patches, rest + 1, classes // 2, 2 * prow, cols), jnp.int16),
             edges, edges, edges, edges,
+            meta, meta, meta, meta,
             pltpu.VMEM((patches, 3, wide, cols), F32),
             pltpu.VMEM((MOST_ACQ, planes + 2, prow, cols), F32),
-            pltpu.SemaphoreType.DMA((2,)),
-            pltpu.SemaphoreType.DMA((2,)),
+            pltpu.SemaphoreType.DMA((6,)),
+            pltpu.SemaphoreType.DMA((4,)),
+            pltpu.SemaphoreType.DMA((4,)),
             pltpu.SemaphoreType.DMA((2 * patches,)),
             pltpu.SemaphoreType.DMA((2 * patches,)),
         ],
         compiler_params=pltpu.CompilerParams(
-            collective_id=0, has_side_effects=True, vmem_limit_bytes=30 * 1024 * 1024
+            collective_id=0, has_side_effects=True, vmem_limit_bytes=56 * 1024 * 1024
         ),
         cost_estimate=pl.CostEstimate(
             flops=2 * cells * wide * 27 * channels,
             bytes_accessed=2 * features.size + 4 * classes * MOST_ACQ * rows * cols,
             transcendentals=cells * folds * classes,
         ),
-    )(features, jnp.swapaxes(conv_weight, 1, 2), norm_gain, norm_bias, jnp.swapaxes(head_weight, 0, 1), head_bias, patch_offsets, fg_mask, acq_counts)
+    )(*operands, patch_offsets, fg_mask, acq_counts)
 
 
 def solution(mesh):

time: 38.4 us -> 36 us (0.938)
  local copies, waits for them, and re-layouts: 4.85 us -> 1.78 us
  Pallas kernels: 32.5 us -> 33.3 us
    unnamed x17 -> x1, local copies, waits for them, and re-layouts: 4.85 us -> 1.78 us
    pallas_call x1, Pallas kernels: 32.5 us -> 33.3 us  [local(): pl.pallas_call(kernel, out_shape=jax.ShapeDtypeStruct((classes, MOST_ACQ,...]
where the time goes in v3:
time: 36 us; the launch traced here: 35.8 us
  Pallas kernels  33.3 us (92%)
  local copies, waits for them, and re-layouts  1.78 us (5%)
  between operations  0.66 us (2%)
    pallas_call x1, Pallas kernels, local(): pl.pallas_call(kernel, out_shape=jax.ShapeDtypeStruct((classes, MOST_ACQ,...  33.3 us
    unnamed x1, local copies, waits for them, and re-layouts  1.78 us

profile of v3, /device:TPU:1, one launch (start us, length us, event | category | flops | bytes accessed | tf_op | source)
XLA Modules:
  0.0 35.8 jit_solution(17460290098861555258)
XLA Ops:
  0.7 33.3 %shard_map.91 = f32[6,8,16,128]{3,2,1,0:T(8,128)} custom-call(bf16[32,6,16,128]{3,2,1,0:T(8,128)(2,1)} %feat_in.1, bf16[3,288,128]{2,1,0:T(8,128)(2,1)} %bitcast.2, f32[4,32]{1,0:T(4,128)} %gain_in.1, f32[4,32]{1,0:T(4,128)} %bias_in.1, bf16[6,4,32]{2,1,0:T(4,128)(2,1)} %bitcast.3, f32[4,6]{1,0:T(4,128)} %hbias_in.1, s32[1,2]{1,0:T(1,128)} %offs.1, ...), custom_call_target="tpu_custom_call" | custom-call | flops 4529848320 | bytes 1179648 | tf_op jit(solution)/shard_map/pallas_call | solution.py:457
  34.0 1.8 %copy.12 = f32[6,8,16,128]{3,2,1,0:T(8,128)} copy(f32[6,8,16,128]{3,2,1,0:T(8,128)} %shard_map.91) | data formatting | bytes 786432

commit v4 on v3

--- a/solution.py
+++ b/solution.py
@@ -322,57 +322,6 @@
         def _():
             remote(snd_lo.at[p], rcv_above.at[p], edge, 2 * p + 1, left).start()
 
-    for p in range(patches):
-        conv_plane(p, 0, RIM + 1)
-        shift_of(p)
-        add_stats(p, 0)
-
-        @pl.loop(1, inner)
-        def _(i, p=p):
-            conv_plane(p, i, RIM + 1 + i)
-            add_stats(p, i)
-
-    @pl.when(has_left)
-    def _():
-        remote(feat_in.at[:, planes - RIM :], before, halo, 0, left).wait_recv()
-        remote(meta_hi, meta_below, halo, 2, left).wait_recv()
-
-    @pl.when(has_right)
-    def _():
-        remote(feat_in.at[:, :RIM], after, halo, 1, right).wait_recv()
-        remote(meta_lo, meta_above, halo, 3, right).wait_recv()
-
-    lay_planes(before, 0, 0, RIM, True)
-    lay_planes(after, 0, RIM + planes, RIM, True)
-
-    def conv_rest(p, t):
-        conv_plane(p, inner + t, starts[p] + rest_index(p, t))
-        add_stats(p, inner + t)
-
-    def score_rest(p, t, norms):
-        score_plane(p, inner + t, rest_index(p, t), *norms, code=t)
-
-    @pl.loop(0, rest)
-    def _(t):
-        conv_rest(0, t)
-
-    norms = []
-    for p in range(patches):
-        norms.append(affine(p))
-
-        @pl.loop(0, rest)
-        def _(t, p=p):
-            if p + 1 < patches:
-                conv_rest(p + 1, t)
-            score_rest(p, t, norms[p])
-
-        send_edges(p)
-
-    @pl.loop(0, inner)
-    def _(i):
-        for p in range(patches):
-            score_plane(p, i, RIM + 1 + i - starts[p], *norms[p])
-
     shape = (prow, cols)
     count = jnp.full(shape, acq[0].astype(F32), F32)
     step = planes / jnp.maximum(count - 1.0, 1.0)
@@ -383,6 +332,67 @@
         for e in range(planes + 2):
             value = jnp.maximum(0.0, 1.0 - jnp.abs(position - (e - 1.0)))
             coef[slot, e] = jnp.where(count > slot, value, 0.0)
+
+    for p in range(patches):
+        conv_plane(p, 0, RIM + 1)
+        shift_of(p)
+        add_stats(p, 0)
+
+    @pl.loop(1, inner)
+    def _(i):
+        for p in range(patches):
+            conv_plane(p, i, RIM + 1 + i)
+            add_stats(p, i)
+
+    @pl.when(has_left)
+    def _():
+        remote(feat_in.at[:, planes - RIM :], before, halo, 0, left).wait_recv()
+        remote(meta_hi, meta_below, halo, 2, left).wait_recv()
+
+    @pl.when(has_right)
+    def _():
+        remote(feat_in.at[:, :RIM], after, halo, 1, right).wait_recv()
+        remote(meta_lo, meta_above, halo, 3, right).wait_recv()
+
+    lay_planes(before, 0, 0, RIM, True)
+    lay_planes(after, 0, RIM + planes, RIM, True)
+
+    def conv_rest(p, t):
+        conv_plane(p, inner + t, starts[p] + rest_index(p, t))
+        add_stats(p, inner + t)
+
+    def score_rest(p, t, norms):
+        score_plane(p, inner + t, rest_index(p, t), *norms, code=t)
+
+    @pl.loop(0, rest)
+    def _(t):
+        conv_rest(0, t)
+
+    norms = []
+    for p in range(patches):
+        norms.append(affine(p))
+
+        if p + 1 < patches:
+
+            @pl.loop(0, rest)
+            def _(t, p=p):
+                conv_rest(p + 1, t)
+                score_rest(p, t, norms[p])
+        else:
+
+            @pl.loop(0, rest // 2)
+            def _(t, p=p):
+                score_rest(p, 2 * t, norms[p])
+                score_rest(p, 2 * t + 1, norms[p])
+            if rest % 2:
+                score_rest(p, rest - 1, norms[p])
+
+        send_edges(p)
+
+    @pl.loop(0, inner)
+    def _(i):
+        for p in range(patches):
+            score_plane(p, i, RIM + 1 + i - starts[p], *norms[p])
 
     for p in range(patches):
 

time: 36 us -> 35.2 us (0.978)
  Pallas kernels: 33.3 us -> 32.6 us
    pallas_call x1, Pallas kernels: 33.3 us -> 32.6 us  [local(): pl.pallas_call(kernel, out_shape=jax.ShapeDtypeStruct((classes, MOST_ACQ,...]
where the time goes in v4:
time: 35.2 us; the launch traced here: 35.1 us
  Pallas kernels  32.6 us (93%)
  local copies, waits for them, and re-layouts  1.78 us (5%)
  between operations  0.66 us (2%)
    pallas_call x1, Pallas kernels, local(): pl.pallas_call(kernel, out_shape=jax.ShapeDtypeStruct((classes, MOST_ACQ,...  32.6 us
    unnamed x1, local copies, waits for them, and re-layouts  1.78 us

profile of v4, /device:TPU:1, one launch (start us, length us, event | category | flops | bytes accessed | tf_op | source)
XLA Modules:
  0.0 35.1 jit_solution(7270974571343082861)
XLA Ops:
  0.7 32.6 %shard_map.91 = f32[6,8,16,128]{3,2,1,0:T(8,128)} custom-call(bf16[32,6,16,128]{3,2,1,0:T(8,128)(2,1)} %feat_in.1, bf16[3,288,128]{2,1,0:T(8,128)(2,1)} %bitcast.2, f32[4,32]{1,0:T(4,128)} %gain_in.1, f32[4,32]{1,0:T(4,128)} %bias_in.1, bf16[6,4,32]{2,1,0:T(4,128)(2,1)} %bitcast.3, f32[4,6]{1,0:T(4,128)} %hbias_in.1, s32[1,2]{1,0:T(1,128)} %offs.1, ...), custom_call_target="tpu_custom_call" | custom-call | flops 4529848320 | bytes 1179648 | tf_op jit(solution)/shard_map/pallas_call | solution.py:467
  33.3 1.8 %copy.12 = f32[6,8,16,128]{3,2,1,0:T(8,128)} copy(f32[6,8,16,128]{3,2,1,0:T(8,128)} %shard_map.91) | data formatting | bytes 786432

commit v5 on v4

--- a/solution.py
+++ b/solution.py
@@ -344,18 +344,32 @@
             conv_plane(p, i, RIM + 1 + i)
             add_stats(p, i)
 
-    @pl.when(has_left)
-    def _():
-        remote(feat_in.at[:, planes - RIM :], before, halo, 0, left).wait_recv()
-        remote(meta_hi, meta_below, halo, 2, left).wait_recv()
-
-    @pl.when(has_right)
-    def _():
-        remote(feat_in.at[:, :RIM], after, halo, 1, right).wait_recv()
-        remote(meta_lo, meta_above, halo, 3, right).wait_recv()
-
-    lay_planes(before, 0, 0, RIM, True)
-    lay_planes(after, 0, RIM + planes, RIM, True)
+    def take_before():
+        @pl.when(has_left)
+        def _():
+            remote(feat_in.at[:, planes - RIM :], before, halo, 0, left).wait_recv()
+            remote(meta_hi, meta_below, halo, 2, left).wait_recv()
+
+        lay_planes(before, 0, 0, RIM, True)
+
+    def take_after():
+        @pl.when(has_right)
+        def _():
+            remote(feat_in.at[:, :RIM], after, halo, 1, right).wait_recv()
+            remote(meta_lo, meta_above, halo, 3, right).wait_recv()
+
+        lay_planes(after, 0, RIM + planes, RIM, True)
+
+    @pl.when(me % 2 == 0)
+    def _():
+        take_after()
+        take_before()
+
+    @pl.when(me % 2 == 1)
+    def _():
+        take_before()
+        take_after()
+
 
     def conv_rest(p, t):
         conv_plane(p, inner + t, starts[p] + rest_index(p, t))

time: 35.2 us -> 34.2 us (0.972)
  Pallas kernels: 32.6 us -> 31.6 us
    pallas_call x1, Pallas kernels: 32.6 us -> 31.6 us  [local(): pl.pallas_call(kernel, out_shape=jax.ShapeDtypeStruct((classes, MOST_ACQ,...]
where the time goes in v5:
time: 34.2 us; the launch traced here: 34.1 us
  Pallas kernels  31.6 us (92%)
  local copies, waits for them, and re-layouts  1.78 us (5%)
  between operations  0.66 us (2%)
    pallas_call x1, Pallas kernels, local(): pl.pallas_call(kernel, out_shape=jax.ShapeDtypeStruct((classes, MOST_ACQ,...  31.6 us
    unnamed x1, local copies, waits for them, and re-layouts  1.78 us

profile of v5, /device:TPU:1, one launch (start us, length us, event | category | flops | bytes accessed | tf_op | source)
XLA Modules:
  0.0 34.1 jit_solution(1817092053183534562)
XLA Ops:
  0.7 31.6 %shard_map.91 = f32[6,8,16,128]{3,2,1,0:T(8,128)} custom-call(bf16[32,6,16,128]{3,2,1,0:T(8,128)(2,1)} %feat_in.1, bf16[3,288,128]{2,1,0:T(8,128)(2,1)} %bitcast.2, f32[4,32]{1,0:T(4,128)} %gain_in.1, f32[4,32]{1,0:T(4,128)} %bias_in.1, bf16[6,4,32]{2,1,0:T(4,128)(2,1)} %bitcast.3, f32[4,6]{1,0:T(4,128)} %hbias_in.1, s32[1,2]{1,0:T(1,128)} %offs.1, ...), custom_call_target="tpu_custom_call" | custom-call | flops 4529848320 | bytes 1179648 | tf_op jit(solution)/shard_map/pallas_call | solution.py:481
  32.3 1.8 %copy.12 = f32[6,8,16,128]{3,2,1,0:T(8,128)} copy(f32[6,8,16,128]{3,2,1,0:T(8,128)} %shard_map.91) | data formatting | bytes 786432
